TPU v7x, 32 devices: a whole 2x2x4 slice. The times are simulated.
32 devices in a mesh: row: 4 (over z), col: 8 (over y, x, core).
Axes of the slice: x: 2, y: 2, z: 4, core: 2. Of those that a mesh axis runs over, the one named last changes fastest.
Arguments:
- tile_values: float32 [4, 8, 128, 128, 128], P('row', 'col')
- tile_coords: int32 [4, 8, 128, 2], P('row', 'col'), may hold values from 0 to 143, as said below
- tile_count: int32 [4, 8], P('row', 'col'), may hold values from 16 to 128, as said below
- objective: float32 [65536], P('col')
- lower: float32 [65536], P('col'), may hold values from -2 to -0.2
- upper: float32 [65536], P('col'), may hold values from 0.2 to 2
- rhs: float32 [73728], P('row')
- primal_start: float32 [65536], P('col'), may hold values from -4 to 4
- dual_start: float32 [73728], P('row'), may hold values from 0 to 1
- step_size: float32 [1], replicated, may hold values from 0.02 to 0.06
Outputs:
- primal_solution: float32 [65536], P('col')
- dual_solution: float32 [73728], P('row')
Inputs may be any that keep to these rules, and one draw needn't show every extreme that they name: `tile_coords`: coordinates are local: block rows 0 to 143, block columns 0 to 63, also in unused slots. Devices whose col index is congruent to their row index modulo the size of row hold one period: their block rows are (col index // size of row) * 64 plus 0 to 63. All other devices hold only linking block rows, 128 to 143. Every block row and every block column of A is met by some used slot. `tile_count`: period devices use all slots; other devices use 16 to 64 slots.
All inputs are finite; a program needn't handle non-finite values.
Results may differ from a plain program's by a relative error of at most 0.00012.
Values sent between devices are 32-bit elements; how exact they have to be, the bound alone decides.
A program may use at most 64 MiB of HBM per device.

v0:
```python
import jax
import jax.numpy as jnp
from jax import lax
from jax.sharding import PartitionSpec as P

RUIZ = 2
ITERS = 2


EPSILON = 1e-06
HIGHEST = lax.Precision.HIGHEST


def local(
    tile_values,
    tile_coords,
    tile_count,
    objective,
    lower,
    upper,
    rhs,
    primal_start,
    dual_start,
    step_size,
):
    tile_width = tile_values.shape[-1]
    slot_count = tile_values.shape[2]
    matrix = tile_values.reshape(slot_count, tile_width, tile_width)
    coords = tile_coords.reshape(slot_count, 2)
    block_rows = coords[:, 0]
    block_cols = coords[:, 1]
    row_blocks = rhs.shape[0] // tile_width
    col_blocks = objective.shape[0] // tile_width
    in_use = (jnp.arange(slot_count, dtype=jnp.int32) < tile_count.reshape(())).astype(jnp.float32)
    row_onehot = (jnp.arange(row_blocks, dtype=jnp.int32)[:, None] == block_rows[None, :]).astype(
        jnp.float32
    ) * in_use[None, :]
    col_onehot = (jnp.arange(col_blocks, dtype=jnp.int32)[:, None] == block_cols[None, :]).astype(
        jnp.float32
    ) * in_use[None, :]
    magnitude = jnp.abs(matrix) * in_use[:, None, None]
    row_scale = jnp.ones((row_blocks, tile_width), jnp.float32)
    col_scale = jnp.ones((col_blocks, tile_width), jnp.float32)
    for sweep in range(RUIZ):
        col_pieces = jnp.take(col_scale, block_cols, axis=0)
        row_pieces = jnp.take(row_scale, block_rows, axis=0)
        row_local = jnp.max(magnitude * col_pieces[:, None, :], axis=2)
        col_local = jnp.max(magnitude * row_pieces[:, :, None], axis=1)
        row_peak = jnp.zeros((row_blocks, tile_width), jnp.float32).at[block_rows].max(row_local)
        col_peak = jnp.zeros((col_blocks, tile_width), jnp.float32).at[block_cols].max(col_local)
        peak_target = row_peak
        peak_joined = lax.pmax(peak_target, "col")
        row_peak = peak_joined
        col_peak = lax.pmax(col_peak, "row")
        row_scale = row_scale / jnp.sqrt(row_scale * row_peak + EPSILON)
        col_scale = col_scale / jnp.sqrt(col_scale * col_peak + EPSILON)
    cost = col_scale * objective.reshape(col_blocks, tile_width)
    bound = row_scale * rhs.reshape(row_blocks, tile_width)
    low_scaled = lower.reshape(col_blocks, tile_width) / col_scale
    high_scaled = upper.reshape(col_blocks, tile_width) / col_scale
    primal = primal_start.reshape(col_blocks, tile_width) / col_scale
    dual = dual_start.reshape(row_blocks, tile_width) / row_scale
    cost_square = jnp.sum(cost * cost)
    bound_square = jnp.sum(bound * bound)
    cost_total = lax.psum(cost_square, "col")
    bound_total = lax.psum(bound_square, "row")
    weight = jnp.sqrt(cost_total + EPSILON) / jnp.sqrt(bound_total + EPSILON)
    primal_step = step_size[0] / weight
    dual_step = step_size[0] * weight
    for iteration in range(ITERS):
        pieces = jnp.take(row_scale * dual, block_rows, axis=0)
        products = jnp.einsum("tij,ti->tj", matrix, pieces, precision=HIGHEST)
        image = lax.psum(jnp.dot(col_onehot, products, precision=HIGHEST), "row")
        moved = jnp.clip(primal - primal_step * (cost - col_scale * image), low_scaled, high_scaled)
        extra = 2.0 * moved - primal
        forward_pieces = jnp.take(col_scale * extra, block_cols, axis=0)
        forward_products = jnp.einsum("tij,tj->ti", matrix, forward_pieces, precision=HIGHEST)
        partial_rows = jnp.dot(row_onehot, forward_products, precision=HIGHEST)
        total = lax.psum(partial_rows, "col")
        dual = jnp.maximum(dual + dual_step * (bound - row_scale * total), 0.0)
        primal = moved
    return ((col_scale * primal).reshape(-1), (row_scale * dual).reshape(-1))


def solution(mesh):
    placed = (
        P("row", "col", None, None, None),
        P("row", "col", None, None),
        P("row", "col"),
        P("col"),
        P("col"),
        P("col"),
        P("row"),
        P("col"),
        P("row"),
        P(),
    )
    return jax.shard_map(
        local, mesh=mesh, in_specs=placed, out_specs=(P("col"), P("row")), check_vma=False
    )
```

profile of v0, /device:TPU:0, one launch (start us, length us, event | category | flops | bytes accessed | tf_op | source)
XLA Modules:
  0.0 340.4 jit_solution(15628616969606805450)
XLA Ops:
  10.2 5.7 %multiply_reduce_fusion.3 = f32[128,128]{1,0:T(8,128)S(1)} fusion(f32[1,1,128,128,128]{4,3,2,1,0:T(8,128)} %param.14, f32[128,128]{1,0:T(8,128)S(1)} %broadcast_select_fusion.7, f32[128]{0:T(128)S(1)} %compare_convert_fusion), kind=kLoop, calls=%fused_computation.25 | loop fusion | flops 8372224 | bytes 8520192 | tf_op jit(solution)/shard_map/reduce_max | solution.py:48
  15.9 1.0 scatter_custom_fusion
  16.9 20.8 %pmax.28 = f32[64,128]{1,0:T(8,128)S(1)} all-reduce(f32[64,128]{1,0:T(8,128)S(1)} %scatter_custom_fusion), channel_id=1, replica_groups=mesh['row'=4,'col'=8] {'row'}, use_global_device_ids=true, to_apply=%region_2.4 | all-reduce | flops 8192 | bytes 65536 | tf_op jit(solution)/shard_map/pmax | solution.py:54
  39.1 7.3 %multiply_reduce_fusion = (f32[128,128]{1,0:T(8,128)S(1)}, f32[128,128]{1,0:T(8,128)S(1)}) fusion(f32[1,1,128,128,128]{4,3,2,1,0:T(8,128)} %param.14, f32[128,128]{1,0:T(8,128)S(1)} %get-tuple-element.30, f32[128]{0:T(128)S(1)} %compare_convert_fusion, f32[128,128]{1,0:T(8,128)S(1)} %get-tuple-element.29), kind=kLoop, calls=%fused_computation.22 | loop fusion | flops 12550144 | bytes 8651264 | tf_op jit(solution)/shard_map/reduce_max | solution.py:47
  46.4 1.6 scatter_custom_fusion.3
  48.0 1.6 scatter_custom_fusion.1
  50.3 49.8 %all-reduce.10.cloned.1.call-done = (f32[144,128]{1,0:T(8,128)}, f32[144,128]{1,0:T(8,128)}) async-done(((f32[144,128]{1,0:T(8,128)}, f32[144,128]{1,0:T(8,128)}), (f32[144,128]{1,0:T(8,128)}, f32[144,128]{1,0:T(8,128)})) %all-reduce.10.cloned.1.call-update) | async-done | bytes 147472 | tf_op jit(solution)/shard_map/pmax | solution.py:52
  100.1 1.6 multiply_reduce_fusion.4
  103.1 9.4 %fusion.6 = f32[128,1,128]{2,1,0:T(1,128)S(1)} fusion(f32[128,128,1]{1,2,0:T(1,128)S(1)} %bitcast.129, f32[1,1,128,128,128]{4,3,2,1,0:T(8,128)} %param.14), kind=kOutput, calls=%fused_computation.18 | convolution fusion | flops 25165824 | bytes 8519680 | tf_op jit(solution)/shard_map/tij,ti->tj/dot_general | solution.py:72
  112.5 5.7 %multiply_reduce_fusion.1 = f32[128,128]{1,0:T(8,128)S(1)} fusion(f32[1,1,128,128,128]{4,3,2,1,0:T(8,128)} %param.14, f32[128,128]{1,0:T(8,128)S(1)} %get-tuple-element.28, f32[128]{0:T(128)S(1)} %compare_convert_fusion), kind=kLoop, calls=%fused_computation.23 | loop fusion | flops 8372224 | bytes 8520192 | tf_op jit(solution)/shard_map/reduce_max | solution.py:48
  118.2 1.0 scatter_custom_fusion.2
  119.2 19.0 %pmax.30 = f32[64,128]{1,0:T(8,128)S(1)} all-reduce(f32[64,128]{1,0:T(8,128)S(1)} %scatter_custom_fusion.2), channel_id=1, replica_groups=mesh['row'=4,'col'=8] {'row'}, use_global_device_ids=true, to_apply=%region_8.11 | all-reduce | flops 8192 | bytes 65536 | tf_op jit(solution)/shard_map/pmax | solution.py:54
  138.9 12.4 %psum.42 = f32[]{:T(128)} all-reduce(f32[]{:T(128)} %get-tuple-element.10), channel_id=1, replica_groups=mesh['row'=4,'col'=8] {'col'}, use_global_device_ids=true, to_apply=%region_10.13 | all-reduce | flops 1 | bytes 8 | tf_op jit(solution)/shard_map/psum | solution.py:65
  152.2 17.2 %all-reduce.1 = (f32[64,128]{1,0:T(8,128)S(1)}, f32[]{:T(128)}) all-reduce(f32[64,128]{1,0:T(8,128)S(1)} %fusion.16, f32[]{:T(128)} %get-tuple-element.12), channel_id=1, replica_groups=mesh['row'=4,'col'=8] {'row'}, use_global_device_ids=true, to_apply=%region_16.19 | all-reduce | flops 8193 | bytes 65544 | tf_op jit(solution)/shard_map/psum | solution.py:73
  171.0 15.4 %fusion.4 = f32[128,1,128]{2,1,0:T(1,128)S(1)} fusion(f32[128,128,1]{1,2,0:T(1,128)S(1)} %bitcast.128, f32[1,1,128,128,128]{4,3,2,1,0:T(8,128)} %param.14), kind=kOutput, calls=%fused_computation.16 | convolution fusion | flops 25165824 | bytes 8519680 | tf_op jit(solution)/shard_map/tij,tj->ti/dot_general | solution.py:77
  186.3 0.9 fusion.11
  187.3 48.9 %all-reduce.6.cloned.1.call-done = f32[144,128]{1,0:T(8,128)} async-done(((f32[144,128]{1,0:T(8,128)}), f32[144,128]{1,0:T(8,128)}) %all-reduce.6.cloned.1.call-update) | async-done | bytes 73744 | tf_op jit(solution)/shard_map/psum | solution.py:79
  236.2 0.9 fusion.13
  237.9 9.4 %fusion.2 = f32[128,1,128]{2,1,0:T(1,128)S(1)} fusion(f32[128,128,1]{1,2,0:T(1,128)S(1)} %bitcast.125, f32[1,1,128,128,128]{4,3,2,1,0:T(8,128)} %param.14), kind=kOutput, calls=%fused_computation.14 | convolution fusion | flops 25165824 | bytes 8519680 | tf_op jit(solution)/shard_map/tij,ti->tj/dot_general | solution.py:72
  247.5 19.0 %psum.46 = f32[64,128]{1,0:T(8,128)S(1)} all-reduce(f32[64,128]{1,0:T(8,128)S(1)} %fusion.14), channel_id=1, replica_groups=mesh['row'=4,'col'=8] {'row'}, use_global_device_ids=true, to_apply=%region_18.21 | all-reduce | flops 8192 | bytes 65536 | tf_op jit(solution)/shard_map/psum | solution.py:73
  267.9 15.4 %fusion = f32[128,1,128]{2,1,0:T(1,128)S(1)} fusion(f32[128,128,1]{1,2,0:T(1,128)S(1)} %bitcast.127, f32[1,1,128,128,128]{4,3,2,1,0:T(8,128)} %param.14), kind=kOutput, calls=%fused_computation.12 | convolution fusion | flops 25165824 | bytes 8519680 | tf_op jit(solution)/shard_map/tij,tj->ti/dot_general | solution.py:77
  283.3 0.8 fusion.9
  284.1 48.1 %all-reduce.8.cloned.1.call-done = f32[144,128]{1,0:T(8,128)} async-done(((f32[144,128]{1,0:T(8,128)}), f32[144,128]{1,0:T(8,128)}) %all-reduce.8.cloned.1.call-update) | async-done | bytes 73744 | tf_op jit(solution)/shard_map/psum | solution.py:79
  332.3 1.6 multiply_bitcast_fusion
  (48 shorter events, 9.1 us)
Async XLA Ops:
  7.2 93.0 %all-reduce.10.cloned.1.call-start = ((), (), s32[]{:S(2)}) async-start(), calls=%async_computation.2 | async-start | bytes 294912 | tf_op jit(solution)/shard_map/pmax | solution.py:52
  10.2 90.0 %copy-start.1 = (f32[18432]{0:T(1024)S(1)}, f32[18432]{0:T(1024)}, u32[]{:S(2)}) copy-start(f32[18432]{0:T(1024)} %param.20) | copy-start | bytes 221188
  10.2 92.1 %copy-start = (f32[18432]{0:T(1024)S(1)}, f32[18432]{0:T(1024)}, u32[]{:S(2)}) copy-start(f32[18432]{0:T(1024)} %param.22) | copy-start | bytes 221188
  49.6 186.6 %all-reduce.6.cloned.1.call-start = ((), (), s32[]{:S(2)}) async-start(), calls=%async_computation | async-start | bytes 147456 | tf_op jit(solution)/shard_map/psum | solution.py:79
  103.1 35.1 %copy-start.2 = (f32[8192]{0:T(1024)S(1)}, f32[8192]{0:T(1024)}, u32[]{:S(2)}) copy-start(f32[8192]{0:T(1024)} %param.17) | copy-start | bytes 98308
  103.1 67.0 %copy-start.4 = (f32[8192]{0:T(1024)S(1)}, f32[8192]{0:T(1024)}, u32[]{:S(2)}) copy-start(f32[8192]{0:T(1024)} %param.19) | copy-start | bytes 98308
  103.1 67.0 %copy-start.5 = (f32[8192]{0:T(1024)S(1)}, f32[8192]{0:T(1024)}, u32[]{:S(2)}) copy-start(f32[8192]{0:T(1024)} %param.18) | copy-start | bytes 98308
  103.1 67.0 %copy-start.6 = (f32[8192]{0:T(1024)S(1)}, f32[8192]{0:T(1024)}, u32[]{:S(2)}) copy-start(f32[8192]{0:T(1024)} %param.21) | copy-start | bytes 98308
  187.2 145.1 %all-reduce.8.cloned.1.call-start = ((), (), s32[]{:S(2)}) async-start(), calls=%async_computation.1 | async-start | bytes 147456 | tf_op jit(solution)/shard_map/psum | solution.py:79
  237.9 94.4 %copy-start.3 = (f32[144,128]{1,0:T(8,128)S(1)}, f32[144,128]{1,0:T(8,128)}, u32[]{:S(2)}) copy-start(f32[144,128]{1,0:T(8,128)} %all-reduce.6.cloned.1.call-done) | copy-start | bytes 221188
Sparse Core Ops, SparseCore 0:
  49.7 50.3 all-reduce.9
  187.3 48.8 all-reduce.5
  284.3 47.9 all-reduce.7
where the time goes:
time: 342 us; the launch traced here: 340 us
  waiting for transfers between devices  147 us (43%)
  blocking collectives  88.4 us (26%)
  matrix products  51.7 us (15%)
  other arithmetic  31.2 us (9%)
  between operations  16.8 us (5%)
  local copies, waits for them, and re-layouts  5.21 us (2%)
    psum x2, waiting for transfers between devices, local(): total = lax.psum(partial_rows, 'col')  97.1 us
    pmax x1, waiting for transfers between devices, local(): peak_joined = lax.pmax(peak_target, 'col')  49.8 us
    pmax x2, blocking collectives, local(): col_peak = lax.pmax(col_peak, 'row')  39.8 us
    psum x2, blocking collectives, local(): image = lax.psum(jnp.dot(col_onehot, products, precision=HIGHEST), 'row')  36.2 us
    dot_general x2, matrix products, local(): jnp.einsum('tij,tj->ti', matrix, forward_pieces, precision=HIGHEST)  30.8 us
    dot_general x2, matrix products, local(): products = jnp.einsum('tij,ti->tj', matrix, pieces, precision=HIGHEST)  18.8 us
    psum x1, blocking collectives, local(): cost_total = lax.psum(cost_square, 'col')  12.4 us
    reduce_max x2, other arithmetic, local(): col_local = jnp.max(magnitude * row_pieces[:, :, None], axis=1)  11.3 us
  transfers between devices with their start and end apart: 3, of which 3 were waited for; matrix products, arithmetic and copies ran while one was open for 0% of the time, Pallas kernels for 0%

commit v1 on v0

v1 whole, which is shorter than its diff:
```python
import functools

import jax
import jax.numpy as jnp
from jax import lax
from jax.experimental import pallas as pl
from jax.experimental.pallas import tpu as pltpu
from jax.sharding import PartitionSpec as P

RUIZ = 2
ITERS = 2
EPSILON = 1e-06
GROUP = 8
F32 = jnp.float32
BF16 = jnp.bfloat16
MESH = pl.DeviceIdType.MESH


def dot(a, b, dims=(1, 0)):
    return lax.dot_general(a, b, (((dims[0],), (dims[1],)), ((), ())), preferred_element_type=F32)


def split2(v):
    high = v.astype(BF16)
    return high, (v - high.astype(F32)).astype(BF16)


def pick(onehot, v, dims=(1, 0)):
    high = v.astype(BF16)
    rest = v - high.astype(F32)
    mid = rest.astype(BF16)
    low = (rest - mid.astype(F32)).astype(BF16)
    return (dot(onehot, high, dims) + dot(onehot, mid, dims)) + dot(onehot, low, dims)


def kernel(
    n_row,
    n_col,
    link,
    values_hbm,
    coords_ref,
    count_ref,
    objective_ref,
    lower_ref,
    upper_ref,
    rhs_ref,
    primal_ref,
    dual_ref,
    step_ref,
    primal_out,
    dual_out,
    tiles,
    halves,
    row_local,
    col_local,
    col_pieces,
    row_columns,
    lhs_pieces,
    products,
    col_box,
    link_box,
    norm_box,
    dual_box,
    load_sem,
    col_send,
    col_recv,
    link_send,
    link_recv,
    norm_send,
    norm_recv,
    dual_send,
    dual_recv,
):
    slots, width = tiles.shape[0], tiles.shape[2]
    cb = objective_ref.shape[0]
    rb = rhs_ref.shape[0]
    periods = n_col // n_row
    link_base = rb - link
    my_row = lax.axis_index("row")
    my_col = lax.axis_index("col")
    is_period = lax.rem(my_col, n_row) == my_row
    my_period = my_col // n_row
    period_base = pl.multiple_of(my_period * cb, cb)
    groups = jnp.where(is_period, slots // GROUP, min(slots, cb) // GROUP)

    def load(g):
        part = pl.ds(pl.multiple_of(g * GROUP, GROUP), GROUP)
        return pltpu.make_async_copy(values_hbm.at[part], tiles.at[part], load_sem.at[g])

    def start_load(g, carry):
        load(g).start()
        return carry

    lax.fori_loop(0, groups, start_load, 0)

    barrier = pltpu.get_barrier_semaphore()
    for d in range(1, n_row):
        pl.semaphore_signal(
            barrier, inc=1, device_id={"row": lax.rem(my_row + d, n_row)}, device_id_type=MESH
        )
    for d in range(1, n_col):
        pl.semaphore_signal(
            barrier, inc=1, device_id={"col": lax.rem(my_col + d, n_col)}, device_id_type=MESH
        )

    def remote(box, send, recv, axis, target, index, source):
        return pltpu.make_async_remote_copy(
            src_ref=box.at[source],
            dst_ref=box.at[source],
            send_sem=send.at[index],
            recv_sem=recv.at[source],
            device_id={axis: target},
            device_id_type=MESH,
        )

    class Exchange:
        def __init__(self, box, send, recv, axis):
            self.n = n_row if axis == "row" else n_col
            self.me = my_row if axis == "row" else my_col
            self.args = (box, send, recv, axis)

        def start(self):
            for d in range(1, self.n):
                remote(*self.args, lax.rem(self.me + d, self.n), d, self.me).start()

        def finish(self):
            for d in range(1, self.n):
                other = lax.rem(self.me + self.n - d, self.n)
                remote(*self.args, other, d, other).wait_recv()
            for d in range(1, self.n):
                remote(*self.args, lax.rem(self.me + d, self.n), d, self.me).wait_send()

    def col_exchange(phase):
        return Exchange(col_box.at[phase], col_send.at[phase], col_recv.at[phase], "row")

    def link_exchange(phase):
        return Exchange(link_box.at[phase], link_send.at[phase], link_recv.at[phase], "col")

    norm_exchange = Exchange(norm_box, norm_send, norm_recv, "col")

    square = (slots, slots)
    lane = lax.broadcasted_iota(jnp.int32, square, 1)
    sublane = lax.broadcasted_iota(jnp.int32, square, 0)
    lane_f = lane.astype(F32)
    used = sublane < count_ref[0, 0]
    block_row = jnp.broadcast_to(coords_ref[:, 0:1], square)
    block_col = jnp.broadcast_to(coords_ref[:, 1:2], square)
    local_row = jnp.where(is_period, block_row - period_base, block_row - (link_base - cb))

    def layout(place):
        place = jnp.where(used, place, 2 * slots - 1)
        onehot = jnp.where(place == lane, 1.0, 0.0)
        place_f = place.astype(F32)
        key = place_f * slots + sublane.astype(F32)
        rank = jnp.sum(jnp.where(key.T < key, 1.0, 0.0), axis=1, keepdims=True)
        order = jnp.where(jnp.broadcast_to(rank, square) == lane_f, 1.0, 0.0).T
        placed = jnp.broadcast_to(jnp.sum(order * place_f.T, axis=1, keepdims=True), square)
        masks = []
        d = 1
        while d < slots:
            masks.append(jnp.where(pltpu.roll(placed, slots - d, axis=0) == placed, 1.0, 0.0))
            d *= 2
        first = (pltpu.roll(placed, 1, axis=0) != placed) | (sublane == 0)
        head = jnp.where((placed == lane_f) & first, 1.0, 0.0).T
        return onehot.astype(BF16), onehot.T.astype(BF16), order.astype(BF16), masks, head.astype(BF16)

    row_pick, row_sum, row_order, row_masks, row_head = layout(local_row)
    col_pick, col_sum, col_order, col_masks, col_head = layout(block_col)

    def segment_max(ordered, masks, head):
        d = 1
        for mask in masks:
            ordered = jnp.maximum(ordered, mask * pltpu.roll(ordered, slots - d, axis=0))
            d *= 2
        return pick(head, ordered)

    row_local[...] = jnp.zeros_like(row_local)
    col_local[...] = jnp.zeros_like(col_local)
    products[...] = jnp.zeros_like(products)
    tile_lane = lax.broadcasted_iota(jnp.int32, (width, slots), 1)

    def first_peaks(g, carry):
        load(g).wait()
        joined = row_local[...]
        for k in range(GROUP):
            t = g * GROUP + k
            tile = tiles[t]
            high, low = split2(tile)
            halves[t, 0:width, :] = high
            halves[t, width : 2 * width, :] = low
            size = jnp.abs(tile)
            col_local[pl.ds(t, 1), :] = jnp.max(size, axis=0, keepdims=True)
            joined = jnp.where(tile_lane == t, jnp.max(size, axis=1, keepdims=True), joined)
        row_local[...] = joined
        return carry

    def next_peaks(g, carry):
        joined = row_local[...]
        columns = row_columns[g]
        for k in range(GROUP):
            t = g * GROUP + k
            size = jnp.abs(tiles[t])
            by_row = size * columns[:, k : k + 1]
            by_col = size * col_pieces[pl.ds(t, 1), :]
            col_local[pl.ds(t, 1), :] = jnp.max(by_row, axis=0, keepdims=True)
            joined = jnp.where(tile_lane == t, jnp.max(by_col, axis=1, keepdims=True), joined)
        row_local[...] = joined
        return carry

    def pad_rows(v):
        return jnp.concatenate([v, jnp.zeros((slots - v.shape[0], width), F32)], axis=0)

    row_scale = jnp.ones((slots, width), F32)
    col_scale = jnp.ones((cb, width), F32)
    for sweep in range(RUIZ):
        if sweep == 0:
            lax.fori_loop(0, groups, first_peaks, 0)
            pl.semaphore_wait(barrier, n_row + n_col - 2)
        else:
            col_pieces[...] = pick(col_pick, pad_rows(col_scale))
            turned = pick(row_pick, row_scale).T
            for g in range(slots // GROUP):
                row_columns[g] = turned[:, g * GROUP : (g + 1) * GROUP]
            lax.fori_loop(0, groups, next_peaks, 0)
        row_peak = segment_max(pick(row_order, row_local[...], (1, 1)), row_masks, row_head)
        col_peak = segment_max(pick(col_order, col_local[...]), col_masks, col_head)
        col_box[sweep, my_row, 0:cb, :] = col_peak[0:cb]
        link_box[sweep, my_col] = row_peak[cb : cb + link]
        col_exchange(sweep).start()
        link_exchange(sweep).start()
        col_exchange(sweep).finish()
        link_exchange(sweep).finish()
        link_peak = functools.reduce(jnp.maximum, [link_box[sweep, c] for c in range(n_col)])
        col_peak = functools.reduce(jnp.maximum, [col_box[sweep, r, 0:cb, :] for r in range(n_row)])
        row_peak = jnp.concatenate([row_peak[0:cb], link_peak, row_peak[cb + link :]], axis=0)
        row_scale = row_scale / jnp.sqrt(row_scale * row_peak + EPSILON)
        col_scale = col_scale / jnp.sqrt(col_scale * col_peak + EPSILON)

    def local_rows(ref):
        return pad_rows(jnp.concatenate([ref[pl.ds(period_base, cb), :], ref[link_base:rb, :]], axis=0))

    cost = col_scale * objective_ref[...]
    bound = row_scale * local_rows(rhs_ref)
    low_scaled = lower_ref[...] / col_scale
    high_scaled = upper_ref[...] / col_scale
    primal = primal_ref[...] / col_scale
    dual = local_rows(dual_ref) / row_scale

    def fold(v):
        return jnp.sum(v.reshape(v.shape[0] // 8, 8, width), axis=0)

    norm_box[my_col, 0:8, :] = fold(cost * cost)
    norm_box[my_col, 8:16, :] = jnp.where(is_period, fold(bound[0:cb] * bound[0:cb]), 0.0)
    norm_exchange.start()

    def put_pieces(onehot, v):
        high, low = split2(v)
        shape = (slots // GROUP, GROUP, width)
        lhs_pieces[...] = jnp.concatenate(
            [dot(onehot, high).reshape(shape), dot(onehot, low).reshape(shape)], axis=1
        ).astype(BF16)

    pair_row = lax.rem(lax.broadcasted_iota(jnp.int32, (2 * GROUP, width), 0), GROUP)

    def adjoint_step(g, carry):
        lhs = lhs_pieces[g]
        both = jnp.concatenate([lhs, lhs], axis=1)
        joined = jnp.zeros((2 * GROUP, width), F32)
        for k in range(GROUP):
            joined = jnp.where(pair_row == k, dot(both, halves[g * GROUP + k]), joined)
        part = pl.ds(pl.multiple_of(g * GROUP, GROUP), GROUP)
        products[part, :] = joined[0:GROUP] + joined[GROUP:]
        return carry

    def forward_step(g, carry):
        lhs = lhs_pieces[g]
        joined = jnp.zeros((2 * GROUP, width), F32)
        for k in range(GROUP):
            pair = dot(lhs, halves[g * GROUP + k], (1, 1))
            joined = jnp.where(pair_row == k, pair[:, 0:width] + pair[:, width:], joined)
        part = pl.ds(pl.multiple_of(g * GROUP, GROUP), GROUP)
        products[part, :] = joined[0:GROUP] + joined[GROUP:]
        return carry

    for iteration in range(ITERS):
        phase = RUIZ + iteration
        put_pieces(row_pick, row_scale * dual)
        lax.fori_loop(0, groups, adjoint_step, 0)
        col_box[phase, my_row, 0:cb, :] = pick(col_sum, products[...])[0:cb]
        if iteration == 0:
            norm_exchange.finish()
            cost_sum = functools.reduce(jnp.add, [norm_box[c, 0:8, :] for c in range(n_col)])
            bound_sum = functools.reduce(jnp.add, [norm_box[c, 8:16, :] for c in range(n_col)])
            link_bound = bound[cb : cb + link]
            col_box[phase, my_row, cb : cb + 8, :] = bound_sum + fold(link_bound * link_bound)
        col_exchange(phase).start()
        col_exchange(phase).finish()
        image = functools.reduce(jnp.add, [col_box[phase, r, 0:cb, :] for r in range(n_row)])
        if iteration == 0:
            bound_sum = functools.reduce(
                jnp.add, [col_box[phase, r, cb : cb + 8, :] for r in range(n_row)]
            )
            cost_total = jnp.sum(cost_sum, keepdims=True)
            bound_total = jnp.sum(bound_sum, keepdims=True)
            weight = jnp.sqrt(cost_total + EPSILON) / jnp.sqrt(bound_total + EPSILON)
            primal_step = step_ref[0] / weight
            dual_step = step_ref[0] * weight
        moved = jnp.clip(primal - primal_step * (cost - col_scale * image), low_scaled, high_scaled)
        put_pieces(col_pick, pad_rows(col_scale * (2.0 * moved - primal)))
        lax.fori_loop(0, groups, forward_step, 0)
        total = pick(row_sum, products[...])
        link_box[phase, my_col] = total[cb : cb + link]
        link_exchange(phase).start()
        primal = moved
        own = jnp.maximum(
            dual[0:cb] + dual_step * (bound[0:cb] - row_scale[0:cb] * total[0:cb]), 0.0
        )
        if iteration == ITERS - 1:

            @pl.when(is_period)
            def _():
                dual_box[my_period] = row_scale[0:cb] * own
                for d in range(1, n_col):
                    pltpu.make_async_remote_copy(
                        src_ref=dual_box.at[my_period],
                        dst_ref=dual_box.at[my_period],
                        send_sem=dual_send.at[d],
                        recv_sem=dual_recv.at[my_period],
                        device_id={"col": lax.rem(my_col + d, n_col)},
                        device_id_type=MESH,
                    ).start()

            primal_out[...] = col_scale * primal
        link_exchange(phase).finish()
        link_total = functools.reduce(jnp.add, [link_box[phase, c] for c in range(n_col)])
        span = slice(cb, cb + link)
        link_dual = jnp.maximum(
            dual[span] + dual_step * (bound[span] - row_scale[span] * link_total), 0.0
        )
        dual = pad_rows(jnp.concatenate([own, link_dual], axis=0))
    dual_out[link_base:rb, :] = (row_scale * dual)[cb : cb + link]
    for p in range(periods):
        owner = p * n_row + my_row

        @pl.when(owner != my_col)
        def _():
            pltpu.make_async_remote_copy(
                src_ref=dual_box.at[p],
                dst_ref=dual_box.at[p],
                send_sem=dual_send.at[0],
                recv_sem=dual_recv.at[p],
                device_id={"col": lax.rem(my_col + 1, n_col)},
                device_id_type=MESH,
            ).wait_recv()

        dual_out[p * cb : (p + 1) * cb, :] = dual_box[p]

    @pl.when(is_period)
    def _():
        for d in range(1, n_col):
            pltpu.make_async_remote_copy(
                src_ref=dual_box.at[my_period],
                dst_ref=dual_box.at[my_period],
                send_sem=dual_send.at[d],
                recv_sem=dual_recv.at[my_period],
                device_id={"col": lax.rem(my_col + d, n_col)},
                device_id_type=MESH,
            ).wait_send()


def local(
    n_row,
    n_col,
    tile_values,
    tile_coords,
    tile_count,
    objective,
    lower,
    upper,
    rhs,
    primal_start,
    dual_start,
    step_size,
):
    width = tile_values.shape[-1]
    slots = tile_values.shape[2]
    cb = objective.shape[0] // width
    rb = rhs.shape[0] // width
    periods = n_col // n_row
    link = rb - periods * cb
    vmem = pl.BlockSpec(memory_space=pltpu.VMEM)
    smem = pl.BlockSpec(memory_space=pltpu.SMEM)
    phases = RUIZ + ITERS
    dma = pltpu.SemaphoreType.DMA
    primal, dual = pl.pallas_call(
        functools.partial(kernel, n_row, n_col, link),
        out_shape=(
            jax.ShapeDtypeStruct((cb, width), F32),
            jax.ShapeDtypeStruct((rb, width), F32),
        ),
        in_specs=[pl.BlockSpec(memory_space=pl.ANY), vmem, smem] + [vmem] * 6 + [smem],
        out_specs=(vmem, vmem),
        scratch_shapes=[
            pltpu.VMEM((slots, width, width), F32),
            pltpu.VMEM((slots, 2 * width, width), BF16),
            pltpu.VMEM((width, slots), F32),
            pltpu.VMEM((slots, width), F32),
            pltpu.VMEM((slots, width), F32),
            pltpu.VMEM((slots // GROUP, width, GROUP), F32),
            pltpu.VMEM((slots // GROUP, 2 * GROUP, width), BF16),
            pltpu.VMEM((slots, width), F32),
            pltpu.VMEM((phases, n_row, cb + 8, width), F32),
            pltpu.VMEM((phases, n_col, link, width), F32),
            pltpu.VMEM((n_col, 16, width), F32),
            pltpu.VMEM((periods, cb, width), F32),
            dma((slots // GROUP,)),
            dma((phases, n_row)),
            dma((phases, n_row)),
            dma((phases, n_col)),
            dma((phases, n_col)),
            dma((n_col,)),
            dma((n_col,)),
            dma((n_col,)),
            dma((periods,)),
        ],
        compiler_params=pltpu.CompilerParams(
            collective_id=0, has_side_effects=True, vmem_limit_bytes=40 * 1024 * 1024
        ),
        name="ruiz_pdhg",
    )(
        tile_values.reshape(slots, width, width),
        tile_coords.reshape(slots, 2),
        tile_count.reshape(1, 1),
        objective.reshape(cb, width),
        lower.reshape(cb, width),
        upper.reshape(cb, width),
        rhs.reshape(rb, width),
        primal_start.reshape(cb, width),
        dual_start.reshape(rb, width),
        step_size,
    )
    return primal.reshape(-1), dual.reshape(-1)


def solution(mesh):
    placed = (
        P("row", "col", None, None, None),
        P("row", "col", None, None),
        P("row", "col"),
        P("col"),
        P("col"),
        P("col"),
        P("row"),
        P("col"),
        P("row"),
        P(),
    )
    return jax.shard_map(
        functools.partial(local, mesh.shape["row"], mesh.shape["col"]),
        mesh=mesh,
        in_specs=placed,
        out_specs=(P("col"), P("row")),
        check_vma=False,
    )
```

time: 342 us -> 69.6 us (0.20)
  waiting for transfers between devices: 147 us -> 0 us
  blocking collectives: 88.4 us -> 0 us
  Pallas kernels: 0 us -> 56.9 us
  matrix products: 51.7 us -> 0 us
  other arithmetic: 31.2 us -> 0 us
  between operations: 16.8 us -> 1.94 us
  local copies, waits for them, and re-layouts: 5.21 us -> 10.2 us
    psum x2 -> x0, waiting for transfers between devices: 97.1 us -> none  [local(): total = lax.psum(partial_rows, 'col')]
    pallas_call x0 -> x1, Pallas kernels: none -> 56.9 us  [local(): pl.pallas_call(functools.partial(kernel, n_row, n_col, link), out_shape=(...]
    dot_general x8 -> x0, matrix products: 51.7 us -> none  [the longest x2 30.8 us: local(): jnp.einsum('tij,tj->ti', matrix, forward_pieces, precision=HIGHEST)]
    pmax x1 -> x0, waiting for transfers between devices: 49.8 us -> none  [local(): peak_joined = lax.pmax(peak_target, 'col')]
    psum x3 -> x0, blocking collectives: 48.6 us -> none  [the longest x2 36.2 us: local(): image = lax.psum(jnp.dot(col_onehot, products, precision=HIGHEST), 'row')]
    pmax x2 -> x0, blocking collectives: 39.8 us -> none  [local(): col_peak = lax.pmax(col_peak, 'row')]
    reduce_max x3 -> x0, other arithmetic: 18.6 us -> none  [the longest x2 11.3 us: local(): col_local = jnp.max(magnitude * row_pieces[:, :, None], axis=1)]
    unnamed x14 -> x17, local copies, waits for them, and re-layouts: 0.04 us -> 10.2 us
  transfers between devices with their start and end apart: 3 -> 0, of which waited for: 3 -> 0; matrix products, arithmetic and copies ran while one was open for 0% -> 0% of each run, Pallas kernels for 0% -> 0%
where the time goes in v1:
time: 69.6 us; the launch traced here: 69 us
  Pallas kernels  56.9 us (82%)
  local copies, waits for them, and re-layouts  10.2 us (15%)
  between operations  1.94 us (3%)
    pallas_call x1, Pallas kernels, local(): pl.pallas_call(functools.partial(kernel, n_row, n_col, link), out_shape=(...  56.9 us
    unnamed x17, local copies, waits for them, and re-layouts  10.2 us

profile of v1, /device:TPU:0, one launch (start us, length us, event | category | flops | bytes accessed | tf_op | source)
XLA Modules:
  0.0 69.0 jit_solution(4727070612539474148)
XLA Ops:
  1.9 0.8 %copy.12 = s32[1,1,128,2]{3,2,1,0:T(8,128)S(1)} copy(s32[1,1,128,2]{2,3,1,0:T(2,128)} %param.11) | data formatting | bytes 2048 | tf_op args[1]
  2.7 0.0 copy-start
  2.7 3.4 %copy-done = f32[1,1,128,128,128]{4,3,2,1,0:T(8,128)S(1)} copy-done((f32[1,1,128,128,128]{4,3,2,1,0:T(8,128)S(1)}, f32[1,1,128,128,128]{4,3,2,1,0:T(8,128)}, u32[]{:S(2)}) %copy-start) | copy-done | bytes 8388632
  6.1 0.0 copy-start.1
  6.1 0.9 %copy-done.1 = f32[18432]{0:T(1024)S(1)} copy-done((f32[18432]{0:T(1024)S(1)}, f32[18432]{0:T(1024)}, u32[]{:S(2)}) %copy-start.1) | copy-done | bytes 73752
  7.0 0.0 copy-start.2
  7.0 0.9 %copy-done.2 = f32[18432]{0:T(1024)S(1)} copy-done((f32[18432]{0:T(1024)S(1)}, f32[18432]{0:T(1024)}, u32[]{:S(2)}) %copy-start.2) | copy-done | bytes 73752
  7.9 0.0 copy-start.3
  7.9 0.8 %copy-done.3 = f32[8192]{0:T(1024)S(1)} copy-done((f32[8192]{0:T(1024)S(1)}, f32[8192]{0:T(1024)}, u32[]{:S(2)}) %copy-start.3) | copy-done | bytes 32792
  8.6 0.0 copy-start.4
  8.6 0.8 %copy-done.4 = f32[8192]{0:T(1024)S(1)} copy-done((f32[8192]{0:T(1024)S(1)}, f32[8192]{0:T(1024)}, u32[]{:S(2)}) %copy-start.4) | copy-done | bytes 32792
  9.4 0.0 copy-start.5
  9.4 0.8 %copy-done.5 = f32[8192]{0:T(1024)S(1)} copy-done((f32[8192]{0:T(1024)S(1)}, f32[8192]{0:T(1024)}, u32[]{:S(2)}) %copy-start.5) | copy-done | bytes 32792
  10.1 0.0 copy-start.6
  10.1 0.8 %copy-done.6 = f32[8192]{0:T(1024)S(1)} copy-done((f32[8192]{0:T(1024)S(1)}, f32[8192]{0:T(1024)}, u32[]{:S(2)}) %copy-start.6) | copy-done | bytes 32792
  10.9 56.9 %ruiz_pdhg.1 = (f32[64,128]{1,0:T(8,128)S(1)}, f32[144,128]{1,0:T(8,128)S(1)}) custom-call(f32[128,128,128]{2,1,0:T(8,128)S(1)} %bitcast.10, s32[128,2]{1,0:T(8,128)S(1)} %bitcast.11, s32[1,1]{1,0:T(1,128)S(6)} %copy.15.count_ref, f32[64,128]{1,0:T(8,128)S(1)} %bitcast.15, f32[64,128]{1,0:T(8,128)S(1)} %bitcast.16, f32[64,128]{1,0:T(8,128)S(1)} %bitcast.17, ...), custom_call_target="tpu_custom_call" | custom-call | tf_op jit(solution)/shard_map/ruiz_pdhg/pallas_call | solution.py:395
  67.8 0.6 copy.17
  68.4 0.6 copy.18
Async XLA Ops:
  2.7 3.4 %copy-start = (f32[1,1,128,128,128]{4,3,2,1,0:T(8,128)S(1)}, f32[1,1,128,128,128]{4,3,2,1,0:T(8,128)}, u32[]{:S(2)}) copy-start(f32[1,1,128,128,128]{4,3,2,1,0:T(8,128)} %param.10) | copy-start | bytes 25165828
  6.1 0.9 %copy-start.1 = (f32[18432]{0:T(1024)S(1)}, f32[18432]{0:T(1024)}, u32[]{:S(2)}) copy-start(f32[18432]{0:T(1024)} %param.16) | copy-start | bytes 221188
  7.0 0.9 %copy-start.2 = (f32[18432]{0:T(1024)S(1)}, f32[18432]{0:T(1024)}, u32[]{:S(2)}) copy-start(f32[18432]{0:T(1024)} %param.18) | copy-start | bytes 221188
  7.9 0.8 %copy-start.3 = (f32[8192]{0:T(1024)S(1)}, f32[8192]{0:T(1024)}, u32[]{:S(2)}) copy-start(f32[8192]{0:T(1024)} %param.13) | copy-start | bytes 98308
  8.6 0.8 %copy-start.4 = (f32[8192]{0:T(1024)S(1)}, f32[8192]{0:T(1024)}, u32[]{:S(2)}) copy-start(f32[8192]{0:T(1024)} %param.14) | copy-start | bytes 98308
  9.4 0.8 %copy-start.5 = (f32[8192]{0:T(1024)S(1)}, f32[8192]{0:T(1024)}, u32[]{:S(2)}) copy-start(f32[8192]{0:T(1024)} %param.15) | copy-start | bytes 98308
  10.1 0.8 %copy-start.6 = (f32[8192]{0:T(1024)S(1)}, f32[8192]{0:T(1024)}, u32[]{:S(2)}) copy-start(f32[8192]{0:T(1024)} %param.17) | copy-start | bytes 98308

commit v2 on v1

--- a/solution.py
+++ b/solution.py
@@ -54,7 +54,7 @@
     row_local,
     col_local,
     col_pieces,
-    row_columns,
+    turned,
     lhs_pieces,
     products,
     col_box,
@@ -185,27 +185,55 @@
         for k in range(GROUP):
             t = g * GROUP + k
             tile = tiles[t]
-            high, low = split2(tile)
-            halves[t, 0:width, :] = high
-            halves[t, width : 2 * width, :] = low
             size = jnp.abs(tile)
             col_local[pl.ds(t, 1), :] = jnp.max(size, axis=0, keepdims=True)
             joined = jnp.where(tile_lane == t, jnp.max(size, axis=1, keepdims=True), joined)
         row_local[...] = joined
         return carry
 
-    def next_peaks(g, carry):
+    spread_shape = (2 * GROUP, GROUP * width)
+    spread = jnp.where(
+        lax.rem(lax.broadcasted_iota(jnp.int32, spread_shape, 0), GROUP)
+        == lax.div(lax.broadcasted_iota(jnp.int32, spread_shape, 1), width),
+        1.0,
+        0.0,
+    ).astype(BF16)
+
+    def next_col_peaks(g, carry):
+        columns = dot(lhs_pieces[g], spread, (0, 0))
+        for k in range(GROUP):
+            t = g * GROUP + k
+            by_row = jnp.abs(tiles[t]) * columns[:, k * width : (k + 1) * width]
+            col_local[pl.ds(t, 1), :] = jnp.max(by_row, axis=0, keepdims=True)
+        return carry
+
+    def next_row_peaks(g, carry):
         joined = row_local[...]
-        columns = row_columns[g]
         for k in range(GROUP):
             t = g * GROUP + k
-            size = jnp.abs(tiles[t])
-            by_row = size * columns[:, k : k + 1]
-            by_col = size * col_pieces[pl.ds(t, 1), :]
-            col_local[pl.ds(t, 1), :] = jnp.max(by_row, axis=0, keepdims=True)
+            by_col = jnp.abs(tiles[t]) * col_pieces[pl.ds(t, 1), :]
             joined = jnp.where(tile_lane == t, jnp.max(by_col, axis=1, keepdims=True), joined)
         row_local[...] = joined
         return carry
+
+    def keep_halves(g, carry):
+        for k in range(GROUP):
+            t = g * GROUP + k
+            halves[t, 0:width, :], halves[t, width : 2 * width, :] = split2(tiles[t])
+        return carry
+
+    def keep_turned(g, carry):
+        for k in range(GROUP):
+            t = g * GROUP + k
+            turned[t, 0:width, :], turned[t, width : 2 * width, :] = split2(tiles[t].T)
+        return carry
+
+    def put_pieces(onehot, v):
+        high, low = split2(v)
+        shape = (slots // GROUP, GROUP, width)
+        lhs_pieces[...] = jnp.concatenate(
+            [dot(onehot, high).reshape(shape), dot(onehot, low).reshape(shape)], axis=1
+        ).astype(BF16)
 
     def pad_rows(v):
         return jnp.concatenate([v, jnp.zeros((slots - v.shape[0], width), F32)], axis=0)
@@ -218,16 +246,28 @@
             pl.semaphore_wait(barrier, n_row + n_col - 2)
         else:
             col_pieces[...] = pick(col_pick, pad_rows(col_scale))
-            turned = pick(row_pick, row_scale).T
-            for g in range(slots // GROUP):
-                row_columns[g] = turned[:, g * GROUP : (g + 1) * GROUP]
-            lax.fori_loop(0, groups, next_peaks, 0)
+
+            @pl.when(jnp.logical_not(is_period))
+            def _():
+                put_pieces(row_pick, row_scale)
+                lax.fori_loop(0, groups, next_col_peaks, 0)
+
+            lax.fori_loop(0, groups, next_row_peaks, 0)
         row_peak = segment_max(pick(row_order, row_local[...], (1, 1)), row_masks, row_head)
         col_peak = segment_max(pick(col_order, col_local[...]), col_masks, col_head)
         col_box[sweep, my_row, 0:cb, :] = col_peak[0:cb]
         link_box[sweep, my_col] = row_peak[cb : cb + link]
         col_exchange(sweep).start()
         link_exchange(sweep).start()
+        if sweep == 0:
+            @pl.when(is_period)
+            def _():
+                put_pieces(row_pick, row_scale / jnp.sqrt(row_scale * row_peak + EPSILON))
+                lax.fori_loop(0, groups, next_col_peaks, 0)
+
+            lax.fori_loop(0, groups, keep_halves, 0)
+        else:
+            lax.fori_loop(0, groups, keep_turned, 0)
         col_exchange(sweep).finish()
         link_exchange(sweep).finish()
         link_peak = functools.reduce(jnp.maximum, [link_box[sweep, c] for c in range(n_col)])
@@ -253,31 +293,14 @@
     norm_box[my_col, 8:16, :] = jnp.where(is_period, fold(bound[0:cb] * bound[0:cb]), 0.0)
     norm_exchange.start()
 
-    def put_pieces(onehot, v):
-        high, low = split2(v)
-        shape = (slots // GROUP, GROUP, width)
-        lhs_pieces[...] = jnp.concatenate(
-            [dot(onehot, high).reshape(shape), dot(onehot, low).reshape(shape)], axis=1
-        ).astype(BF16)
-
     pair_row = lax.rem(lax.broadcasted_iota(jnp.int32, (2 * GROUP, width), 0), GROUP)
 
-    def adjoint_step(g, carry):
+    def product_step(weights, g, carry):
         lhs = lhs_pieces[g]
         both = jnp.concatenate([lhs, lhs], axis=1)
         joined = jnp.zeros((2 * GROUP, width), F32)
         for k in range(GROUP):
-            joined = jnp.where(pair_row == k, dot(both, halves[g * GROUP + k]), joined)
-        part = pl.ds(pl.multiple_of(g * GROUP, GROUP), GROUP)
-        products[part, :] = joined[0:GROUP] + joined[GROUP:]
-        return carry
-
-    def forward_step(g, carry):
-        lhs = lhs_pieces[g]
-        joined = jnp.zeros((2 * GROUP, width), F32)
-        for k in range(GROUP):
-            pair = dot(lhs, halves[g * GROUP + k], (1, 1))
-            joined = jnp.where(pair_row == k, pair[:, 0:width] + pair[:, width:], joined)
+            joined = jnp.where(pair_row == k, dot(both, weights[g * GROUP + k]), joined)
         part = pl.ds(pl.multiple_of(g * GROUP, GROUP), GROUP)
         products[part, :] = joined[0:GROUP] + joined[GROUP:]
         return carry
@@ -285,7 +308,7 @@
     for iteration in range(ITERS):
         phase = RUIZ + iteration
         put_pieces(row_pick, row_scale * dual)
-        lax.fori_loop(0, groups, adjoint_step, 0)
+        lax.fori_loop(0, groups, functools.partial(product_step, halves), 0)
         col_box[phase, my_row, 0:cb, :] = pick(col_sum, products[...])[0:cb]
         if iteration == 0:
             norm_exchange.finish()
@@ -307,7 +330,7 @@
             dual_step = step_ref[0] * weight
         moved = jnp.clip(primal - primal_step * (cost - col_scale * image), low_scaled, high_scaled)
         put_pieces(col_pick, pad_rows(col_scale * (2.0 * moved - primal)))
-        lax.fori_loop(0, groups, forward_step, 0)
+        lax.fori_loop(0, groups, functools.partial(product_step, turned), 0)
         total = pick(row_sum, products[...])
         link_box[phase, my_col] = total[cb : cb + link]
         link_exchange(phase).start()
@@ -406,7 +429,7 @@
             pltpu.VMEM((width, slots), F32),
             pltpu.VMEM((slots, width), F32),
             pltpu.VMEM((slots, width), F32),
-            pltpu.VMEM((slots // GROUP, width, GROUP), F32),
+            pltpu.VMEM((slots, 2 * width, width), BF16),
             pltpu.VMEM((slots // GROUP, 2 * GROUP, width), BF16),
             pltpu.VMEM((slots, width), F32),
             pltpu.VMEM((phases, n_row, cb + 8, width), F32),
@@ -424,7 +447,7 @@
             dma((periods,)),
         ],
         compiler_params=pltpu.CompilerParams(
-            collective_id=0, has_side_effects=True, vmem_limit_bytes=40 * 1024 * 1024
+            collective_id=0, has_side_effects=True, vmem_limit_bytes=48 * 1024 * 1024
         ),
         name="ruiz_pdhg",
     )(

time: 69.6 us -> 60.3 us (0.87)
  Pallas kernels: 56.9 us -> 51 us
  local copies, waits for them, and re-layouts: 10.2 us -> 6.83 us
    pallas_call x1, Pallas kernels: 56.9 us -> 51 us  [local(): pl.pallas_call(functools.partial(kernel, n_row, n_col, link), out_shape=(...]
    unnamed x17 -> x15, local copies, waits for them, and re-layouts: 10.2 us -> 6.83 us
where the time goes in v2:
time: 60.3 us; the launch traced here: 59.8 us
  Pallas kernels  51 us (85%)
  local copies, waits for them, and re-layouts  6.83 us (11%)
  between operations  1.94 us (3%)
    pallas_call x1, Pallas kernels, local(): pl.pallas_call(functools.partial(kernel, n_row, n_col, link), out_shape=(...  51 us
    unnamed x15, local copies, waits for them, and re-layouts  6.83 us

profile of v2, /device:TPU:0, one launch (start us, length us, event | category | flops | bytes accessed | tf_op | source)
XLA Modules:
  0.0 59.8 jit_solution(5473496961258447256)
XLA Ops:
  1.9 0.8 %copy.12 = s32[1,1,128,2]{3,2,1,0:T(8,128)S(1)} copy(s32[1,1,128,2]{2,3,1,0:T(2,128)} %param.11) | data formatting | bytes 2048 | tf_op args[1]
  2.7 0.0 copy-start
  2.7 0.9 %copy-done = f32[18432]{0:T(1024)S(1)} copy-done((f32[18432]{0:T(1024)S(1)}, f32[18432]{0:T(1024)}, u32[]{:S(2)}) %copy-start) | copy-done | bytes 73752
  3.6 0.0 copy-start.1
  3.6 0.9 %copy-done.1 = f32[18432]{0:T(1024)S(1)} copy-done((f32[18432]{0:T(1024)S(1)}, f32[18432]{0:T(1024)}, u32[]{:S(2)}) %copy-start.1) | copy-done | bytes 73752
  4.5 0.0 copy-start.2
  4.5 0.8 %copy-done.2 = f32[8192]{0:T(1024)S(1)} copy-done((f32[8192]{0:T(1024)S(1)}, f32[8192]{0:T(1024)}, u32[]{:S(2)}) %copy-start.2) | copy-done | bytes 32792
  5.2 0.0 copy-start.3
  5.2 0.8 %copy-done.3 = f32[8192]{0:T(1024)S(1)} copy-done((f32[8192]{0:T(1024)S(1)}, f32[8192]{0:T(1024)}, u32[]{:S(2)}) %copy-start.3) | copy-done | bytes 32792
  6.0 0.0 copy-start.4
  6.0 0.8 %copy-done.4 = f32[8192]{0:T(1024)S(1)} copy-done((f32[8192]{0:T(1024)S(1)}, f32[8192]{0:T(1024)}, u32[]{:S(2)}) %copy-start.4) | copy-done | bytes 32792
  6.8 0.0 copy-start.5
  6.8 0.8 %copy-done.5 = f32[8192]{0:T(1024)S(1)} copy-done((f32[8192]{0:T(1024)S(1)}, f32[8192]{0:T(1024)}, u32[]{:S(2)}) %copy-start.5) | copy-done | bytes 32792
  7.5 51.0 %ruiz_pdhg.1 = (f32[64,128]{1,0:T(8,128)S(1)}, f32[144,128]{1,0:T(8,128)S(1)}) custom-call(f32[128,128,128]{2,1,0:T(8,128)} %bitcast.19, s32[128,2]{1,0:T(8,128)S(1)} %bitcast.10, s32[1,1]{1,0:T(1,128)S(6)} %copy.15.count_ref, f32[64,128]{1,0:T(8,128)S(1)} %bitcast.14, f32[64,128]{1,0:T(8,128)S(1)} %bitcast.15, f32[64,128]{1,0:T(8,128)S(1)} %bitcast.16, ...), custom_call_target="tpu_custom_call" | custom-call | tf_op jit(solution)/shard_map/ruiz_pdhg/pallas_call | solution.py:418
  58.5 0.6 %copy.17 = f32[8192]{0:T(1024)} copy(f32[8192]{0:T(1024)S(1)} %bitcast.18) | data formatting | bytes 65536
  59.2 0.6 %copy.18 = f32[18432]{0:T(1024)} copy(f32[18432]{0:T(1024)S(1)} %bitcast.13) | data formatting | bytes 147456
Async XLA Ops:
  2.7 0.9 %copy-start = (f32[18432]{0:T(1024)S(1)}, f32[18432]{0:T(1024)}, u32[]{:S(2)}) copy-start(f32[18432]{0:T(1024)} %param.16) | copy-start | bytes 221188
  3.6 0.9 %copy-start.1 = (f32[18432]{0:T(1024)S(1)}, f32[18432]{0:T(1024)}, u32[]{:S(2)}) copy-start(f32[18432]{0:T(1024)} %param.18) | copy-start | bytes 221188
  4.5 0.8 %copy-start.2 = (f32[8192]{0:T(1024)S(1)}, f32[8192]{0:T(1024)}, u32[]{:S(2)}) copy-start(f32[8192]{0:T(1024)} %param.13) | copy-start | bytes 98308
  5.2 0.8 %copy-start.3 = (f32[8192]{0:T(1024)S(1)}, f32[8192]{0:T(1024)}, u32[]{:S(2)}) copy-start(f32[8192]{0:T(1024)} %param.14) | copy-start | bytes 98308
  6.0 0.8 %copy-start.4 = (f32[8192]{0:T(1024)S(1)}, f32[8192]{0:T(1024)}, u32[]{:S(2)}) copy-start(f32[8192]{0:T(1024)} %param.15) | copy-start | bytes 98308
  6.8 0.8 %copy-start.5 = (f32[8192]{0:T(1024)S(1)}, f32[8192]{0:T(1024)}, u32[]{:S(2)}) copy-start(f32[8192]{0:T(1024)} %param.17) | copy-start | bytes 98308

commit v3 on v2

--- a/solution.py
+++ b/solution.py
@@ -38,14 +38,14 @@
     n_col,
     link,
     values_hbm,
-    coords_ref,
+    coords_hbm,
     count_ref,
-    objective_ref,
-    lower_ref,
-    upper_ref,
-    rhs_ref,
-    primal_ref,
-    dual_ref,
+    objective_hbm,
+    lower_hbm,
+    upper_hbm,
+    rhs_hbm,
+    primal_hbm,
+    dual_hbm,
     step_ref,
     primal_out,
     dual_out,
@@ -61,6 +61,14 @@
     link_box,
     norm_box,
     dual_box,
+    coords_ref,
+    objective_ref,
+    lower_ref,
+    upper_ref,
+    rhs_ref,
+    primal_ref,
+    dual_ref,
+    input_sem,
     load_sem,
     col_send,
     col_recv,
@@ -83,6 +91,23 @@
     period_base = pl.multiple_of(my_period * cb, cb)
     groups = jnp.where(is_period, slots // GROUP, min(slots, cb) // GROUP)
 
+    staged = [
+        pltpu.make_async_copy(source, target, input_sem.at[i])
+        for i, (source, target) in enumerate(
+            (
+                (coords_hbm, coords_ref),
+                (objective_hbm, objective_ref),
+                (lower_hbm, lower_ref),
+                (upper_hbm, upper_ref),
+                (rhs_hbm, rhs_ref),
+                (primal_hbm, primal_ref),
+                (dual_hbm, dual_ref),
+            )
+        )
+    ]
+    for copy in staged[:1]:
+        copy.start()
+
     def load(g):
         part = pl.ds(pl.multiple_of(g * GROUP, GROUP), GROUP)
         return pltpu.make_async_copy(values_hbm.at[part], tiles.at[part], load_sem.at[g])
@@ -92,6 +117,8 @@
         return carry
 
     lax.fori_loop(0, groups, start_load, 0)
+    for copy in staged[1:]:
+        copy.start()
 
     barrier = pltpu.get_barrier_semaphore()
     for d in range(1, n_row):
@@ -127,6 +154,8 @@
             for d in range(1, self.n):
                 other = lax.rem(self.me + self.n - d, self.n)
                 remote(*self.args, other, d, other).wait_recv()
+
+        def drain(self):
             for d in range(1, self.n):
                 remote(*self.args, lax.rem(self.me + d, self.n), d, self.me).wait_send()
 
@@ -142,9 +171,12 @@
     lane = lax.broadcasted_iota(jnp.int32, square, 1)
     sublane = lax.broadcasted_iota(jnp.int32, square, 0)
     lane_f = lane.astype(F32)
+    for copy in staged[:1]:
+        copy.wait()
     used = sublane < count_ref[0, 0]
-    block_row = jnp.broadcast_to(coords_ref[:, 0:1], square)
-    block_col = jnp.broadcast_to(coords_ref[:, 1:2], square)
+    coords = coords_ref[...].astype(F32)
+    block_row = jnp.broadcast_to(coords[0:1, :], square).T.astype(jnp.int32)
+    block_col = jnp.broadcast_to(coords[1:2, :], square).T.astype(jnp.int32)
     local_row = jnp.where(is_period, block_row - period_base, block_row - (link_base - cb))
 
     def layout(place):
@@ -279,6 +311,8 @@
     def local_rows(ref):
         return pad_rows(jnp.concatenate([ref[pl.ds(period_base, cb), :], ref[link_base:rb, :]], axis=0))
 
+    for copy in staged[1:]:
+        copy.wait()
     cost = col_scale * objective_ref[...]
     bound = row_scale * local_rows(rhs_ref)
     low_scaled = lower_ref[...] / col_scale
@@ -378,6 +412,11 @@
 
         dual_out[p * cb : (p + 1) * cb, :] = dual_box[p]
 
+    for phase in range(RUIZ + ITERS):
+        col_exchange(phase).drain()
+        link_exchange(phase).drain()
+    norm_exchange.drain()
+
     @pl.when(is_period)
     def _():
         for d in range(1, n_col):
@@ -411,8 +450,9 @@
     rb = rhs.shape[0] // width
     periods = n_col // n_row
     link = rb - periods * cb
+    smem = pl.BlockSpec(memory_space=pltpu.SMEM)
+    hbm = pl.BlockSpec(memory_space=pltpu.HBM)
     vmem = pl.BlockSpec(memory_space=pltpu.VMEM)
-    smem = pl.BlockSpec(memory_space=pltpu.SMEM)
     phases = RUIZ + ITERS
     dma = pltpu.SemaphoreType.DMA
     primal, dual = pl.pallas_call(
@@ -421,7 +461,7 @@
             jax.ShapeDtypeStruct((cb, width), F32),
             jax.ShapeDtypeStruct((rb, width), F32),
         ),
-        in_specs=[pl.BlockSpec(memory_space=pl.ANY), vmem, smem] + [vmem] * 6 + [smem],
+        in_specs=[hbm, hbm, smem] + [hbm] * 6 + [smem],
         out_specs=(vmem, vmem),
         scratch_shapes=[
             pltpu.VMEM((slots, width, width), F32),
@@ -436,6 +476,14 @@
             pltpu.VMEM((phases, n_col, link, width), F32),
             pltpu.VMEM((n_col, 16, width), F32),
             pltpu.VMEM((periods, cb, width), F32),
+            pltpu.VMEM((2, slots), jnp.int32),
+            pltpu.VMEM((cb, width), F32),
+            pltpu.VMEM((cb, width), F32),
+            pltpu.VMEM((cb, width), F32),
+            pltpu.VMEM((rb, width), F32),
+            pltpu.VMEM((cb, width), F32),
+            pltpu.VMEM((rb, width), F32),
+            dma((7,)),
             dma((slots // GROUP,)),
             dma((phases, n_row)),
             dma((phases, n_row)),
@@ -447,12 +495,12 @@
             dma((periods,)),
         ],
         compiler_params=pltpu.CompilerParams(
-            collective_id=0, has_side_effects=True, vmem_limit_bytes=48 * 1024 * 1024
+            collective_id=0, has_side_effects=True, vmem_limit_bytes=60 * 1024 * 1024
         ),
         name="ruiz_pdhg",
     )(
         tile_values.reshape(slots, width, width),
-        tile_coords.reshape(slots, 2),
+        tile_coords.reshape(slots, 2).T,
         tile_count.reshape(1, 1),
         objective.reshape(cb, width),
         lower.reshape(cb, width),

time: 60.3 us -> 57 us (0.945)
  local copies, waits for them, and re-layouts: 6.83 us -> 2.9 us
  Pallas kernels: 51 us -> 51.9 us
    unnamed x15 -> x2, local copies, waits for them, and re-layouts: 6.83 us -> 2.9 us
    pallas_call x1, Pallas kernels: 51 us -> 51.9 us  [local(): pl.pallas_call(functools.partial(kernel, n_row, n_col, link), out_shape=(...]
where the time goes in v3:
time: 57 us; the launch traced here: 56.7 us
  Pallas kernels  51.9 us (91%)
  local copies, waits for them, and re-layouts  2.9 us (5%)
  between operations  1.93 us (3%)
    pallas_call x1, Pallas kernels, local(): pl.pallas_call(functools.partial(kernel, n_row, n_col, link), out_shape=(...  51.9 us
    unnamed x2, local copies, waits for them, and re-layouts  2.9 us

profile of v3, /device:TPU:0, one launch (start us, length us, event | category | flops | bytes accessed | tf_op | source)
XLA Modules:
  0.0 56.7 jit_solution(12432613905734668438)
XLA Ops:
  1.9 51.9 %ruiz_pdhg.1 = (f32[64,128]{1,0:T(8,128)}, f32[144,128]{1,0:T(8,128)}) custom-call(f32[128,128,128]{2,1,0:T(8,128)} %bitcast.12, s32[2,128]{1,0:T(2,128)} %bitcast.21, s32[1,1]{1,0:T(1,128)S(6)} %copy.14.count_ref, f32[64,128]{1,0:T(8,128)} %bitcast.16, f32[64,128]{1,0:T(8,128)} %bitcast.17, f32[64,128]{1,0:T(8,128)} %bitcast.18, f32[144,128]{1,0:T(8,128)} %bitcast.13, ...), custom_call_target="tpu_custom_call" | custom-call | tf_op jit(solution)/shard_map/ruiz_pdhg/pallas_call | solution.py:458
  53.8 1.4 %copy.16 = f32[8192]{0:T(1024)} copy(f32[8192]{0:T(1024)} %bitcast.20) | data formatting | bytes 65536
  55.2 1.5 %copy.17 = f32[18432]{0:T(1024)} copy(f32[18432]{0:T(1024)} %bitcast.15) | data formatting | bytes 147456

commit v4 on v3

--- a/solution.py
+++ b/solution.py
@@ -267,66 +267,6 @@
             [dot(onehot, high).reshape(shape), dot(onehot, low).reshape(shape)], axis=1
         ).astype(BF16)
 
-    def pad_rows(v):
-        return jnp.concatenate([v, jnp.zeros((slots - v.shape[0], width), F32)], axis=0)
-
-    row_scale = jnp.ones((slots, width), F32)
-    col_scale = jnp.ones((cb, width), F32)
-    for sweep in range(RUIZ):
-        if sweep == 0:
-            lax.fori_loop(0, groups, first_peaks, 0)
-            pl.semaphore_wait(barrier, n_row + n_col - 2)
-        else:
-            col_pieces[...] = pick(col_pick, pad_rows(col_scale))
-
-            @pl.when(jnp.logical_not(is_period))
-            def _():
-                put_pieces(row_pick, row_scale)
-                lax.fori_loop(0, groups, next_col_peaks, 0)
-
-            lax.fori_loop(0, groups, next_row_peaks, 0)
-        row_peak = segment_max(pick(row_order, row_local[...], (1, 1)), row_masks, row_head)
-        col_peak = segment_max(pick(col_order, col_local[...]), col_masks, col_head)
-        col_box[sweep, my_row, 0:cb, :] = col_peak[0:cb]
-        link_box[sweep, my_col] = row_peak[cb : cb + link]
-        col_exchange(sweep).start()
-        link_exchange(sweep).start()
-        if sweep == 0:
-            @pl.when(is_period)
-            def _():
-                put_pieces(row_pick, row_scale / jnp.sqrt(row_scale * row_peak + EPSILON))
-                lax.fori_loop(0, groups, next_col_peaks, 0)
-
-            lax.fori_loop(0, groups, keep_halves, 0)
-        else:
-            lax.fori_loop(0, groups, keep_turned, 0)
-        col_exchange(sweep).finish()
-        link_exchange(sweep).finish()
-        link_peak = functools.reduce(jnp.maximum, [link_box[sweep, c] for c in range(n_col)])
-        col_peak = functools.reduce(jnp.maximum, [col_box[sweep, r, 0:cb, :] for r in range(n_row)])
-        row_peak = jnp.concatenate([row_peak[0:cb], link_peak, row_peak[cb + link :]], axis=0)
-        row_scale = row_scale / jnp.sqrt(row_scale * row_peak + EPSILON)
-        col_scale = col_scale / jnp.sqrt(col_scale * col_peak + EPSILON)
-
-    def local_rows(ref):
-        return pad_rows(jnp.concatenate([ref[pl.ds(period_base, cb), :], ref[link_base:rb, :]], axis=0))
-
-    for copy in staged[1:]:
-        copy.wait()
-    cost = col_scale * objective_ref[...]
-    bound = row_scale * local_rows(rhs_ref)
-    low_scaled = lower_ref[...] / col_scale
-    high_scaled = upper_ref[...] / col_scale
-    primal = primal_ref[...] / col_scale
-    dual = local_rows(dual_ref) / row_scale
-
-    def fold(v):
-        return jnp.sum(v.reshape(v.shape[0] // 8, 8, width), axis=0)
-
-    norm_box[my_col, 0:8, :] = fold(cost * cost)
-    norm_box[my_col, 8:16, :] = jnp.where(is_period, fold(bound[0:cb] * bound[0:cb]), 0.0)
-    norm_exchange.start()
-
     pair_row = lax.rem(lax.broadcasted_iota(jnp.int32, (2 * GROUP, width), 0), GROUP)
 
     def product_step(weights, g, carry):
@@ -339,23 +279,94 @@
         products[part, :] = joined[0:GROUP] + joined[GROUP:]
         return carry
 
+    def pad_rows(v):
+        return jnp.concatenate([v, jnp.zeros((slots - v.shape[0], width), F32)], axis=0)
+
+    def local_rows(ref):
+        return pad_rows(jnp.concatenate([ref[pl.ds(period_base, cb), :], ref[link_base:rb, :]], axis=0))
+
+    def fold(v):
+        return jnp.sum(v.reshape(v.shape[0] // 8, 8, width), axis=0)
+
+    row_scale = jnp.ones((slots, width), F32)
+    col_scale = jnp.ones((cb, width), F32)
+    for sweep in range(RUIZ):
+        if sweep == 0:
+            lax.fori_loop(0, groups, first_peaks, 0)
+            pl.semaphore_wait(barrier, n_row + n_col - 2)
+            for copy in staged[1:]:
+                copy.wait()
+        else:
+            col_pieces[...] = pick(col_pick, pad_rows(col_scale))
+
+            @pl.when(jnp.logical_not(is_period))
+            def _():
+                put_pieces(row_pick, row_scale)
+                lax.fori_loop(0, groups, next_col_peaks, 0)
+
+            lax.fori_loop(0, groups, next_row_peaks, 0)
+        row_peak = segment_max(pick(row_order, row_local[...], (1, 1)), row_masks, row_head)
+        col_peak = segment_max(pick(col_order, col_local[...]), col_masks, col_head)
+        col_box[sweep, my_row, 0:cb, :] = col_peak[0:cb]
+        link_box[sweep, my_col] = row_peak[cb : cb + link]
+        if sweep == RUIZ - 1:
+            known = row_scale[0:cb] / jnp.sqrt(row_scale[0:cb] * row_peak[0:cb] + EPSILON)
+            known = known * rhs_ref[pl.ds(period_base, cb), :]
+            col_box[sweep, my_row, cb : cb + 8, :] = jnp.where(is_period, fold(known * known), 0.0)
+        col_exchange(sweep).start()
+        link_exchange(sweep).start()
+        if sweep == 0:
+            @pl.when(is_period)
+            def _():
+                put_pieces(row_pick, row_scale / jnp.sqrt(row_scale * row_peak + EPSILON))
+                lax.fori_loop(0, groups, next_col_peaks, 0)
+
+            lax.fori_loop(0, groups, keep_halves, 0)
+        else:
+            lax.fori_loop(0, groups, keep_turned, 0)
+            put_pieces(row_pick, local_rows(dual_ref))
+            lax.fori_loop(0, groups, functools.partial(product_step, halves), 0)
+            col_box[RUIZ, my_row, 0:cb, :] = pick(col_sum, products[...])[0:cb]
+        col_exchange(sweep).finish()
+        link_exchange(sweep).finish()
+        link_peak = functools.reduce(jnp.maximum, [link_box[sweep, c] for c in range(n_col)])
+        col_peak = functools.reduce(jnp.maximum, [col_box[sweep, r, 0:cb, :] for r in range(n_row)])
+        row_peak = jnp.concatenate([row_peak[0:cb], link_peak, row_peak[cb + link :]], axis=0)
+        row_scale = row_scale / jnp.sqrt(row_scale * row_peak + EPSILON)
+        col_scale = col_scale / jnp.sqrt(col_scale * col_peak + EPSILON)
+
+    cost = col_scale * objective_ref[...]
+    bound = row_scale * local_rows(rhs_ref)
+    low_scaled = lower_ref[...] / col_scale
+    high_scaled = upper_ref[...] / col_scale
+    primal = primal_ref[...] / col_scale
+    dual = local_rows(dual_ref) / row_scale
+
+    norm_box[my_col, 0:8, :] = fold(cost * cost)
+    norm_box[my_col, 8:16, :] = functools.reduce(
+        jnp.add, [col_box[RUIZ - 1, r, cb : cb + 8, :] for r in range(n_row)]
+    )
+    norm_exchange.start()
+
     for iteration in range(ITERS):
         phase = RUIZ + iteration
-        put_pieces(row_pick, row_scale * dual)
-        lax.fori_loop(0, groups, functools.partial(product_step, halves), 0)
-        col_box[phase, my_row, 0:cb, :] = pick(col_sum, products[...])[0:cb]
         if iteration == 0:
-            norm_exchange.finish()
-            cost_sum = functools.reduce(jnp.add, [norm_box[c, 0:8, :] for c in range(n_col)])
-            bound_sum = functools.reduce(jnp.add, [norm_box[c, 8:16, :] for c in range(n_col)])
             link_bound = bound[cb : cb + link]
-            col_box[phase, my_row, cb : cb + 8, :] = bound_sum + fold(link_bound * link_bound)
+            col_box[phase, my_row, cb : cb + 8, :] = fold(link_bound * link_bound)
+        else:
+            put_pieces(row_pick, row_scale * dual)
+            lax.fori_loop(0, groups, functools.partial(product_step, halves), 0)
+            col_box[phase, my_row, 0:cb, :] = pick(col_sum, products[...])[0:cb]
         col_exchange(phase).start()
         col_exchange(phase).finish()
         image = functools.reduce(jnp.add, [col_box[phase, r, 0:cb, :] for r in range(n_row)])
         if iteration == 0:
+            norm_exchange.finish()
+            cost_sum = functools.reduce(jnp.add, [norm_box[c, 0:8, :] for c in range(n_col)])
             bound_sum = functools.reduce(
-                jnp.add, [col_box[phase, r, cb : cb + 8, :] for r in range(n_row)]
+                jnp.add,
+                [norm_box[c, 8:16, :] for c in range(n_col)]
+                + [col_box[phase, r, cb : cb + 8, :] for r in range(n_row)],
             )
             cost_total = jnp.sum(cost_sum, keepdims=True)
             bound_total = jnp.sum(bound_sum, keepdims=True)

time: 57 us -> 54.4 us (0.954)
  Pallas kernels: 51.9 us -> 49.4 us
    pallas_call x1, Pallas kernels: 51.9 us -> 49.4 us  [local(): pl.pallas_call(functools.partial(kernel, n_row, n_col, link), out_shape=(...]
where the time goes in v4:
time: 54.4 us; the launch traced here: 54.2 us
  Pallas kernels  49.4 us (91%)
  local copies, waits for them, and re-layouts  2.9 us (5%)
  between operations  1.93 us (4%)
    pallas_call x1, Pallas kernels, local(): pl.pallas_call(functools.partial(kernel, n_row, n_col, link), out_shape=(...  49.4 us
    unnamed x2, local copies, waits for them, and re-layouts  2.9 us

profile of v4, /device:TPU:0, one launch (start us, length us, event | category | flops | bytes accessed | tf_op | source)
XLA Modules:
  0.0 54.2 jit_solution(2967696673527335085)
XLA Ops:
  1.9 49.4 %ruiz_pdhg.1 = (f32[64,128]{1,0:T(8,128)}, f32[144,128]{1,0:T(8,128)}) custom-call(f32[128,128,128]{2,1,0:T(8,128)} %bitcast.12, s32[2,128]{1,0:T(2,128)} %bitcast.21, s32[1,1]{1,0:T(1,128)S(6)} %copy.14.count_ref, f32[64,128]{1,0:T(8,128)} %bitcast.16, f32[64,128]{1,0:T(8,128)} %bitcast.17, f32[64,128]{1,0:T(8,128)} %bitcast.18, f32[144,128]{1,0:T(8,128)} %bitcast.13, ...), custom_call_target="tpu_custom_call" | custom-call | tf_op jit(solution)/shard_map/ruiz_pdhg/pallas_call | solution.py:469
  51.3 1.4 %copy.16 = f32[8192]{0:T(1024)} copy(f32[8192]{0:T(1024)} %bitcast.20) | data formatting | bytes 65536
  52.7 1.5 %copy.17 = f32[18432]{0:T(1024)} copy(f32[18432]{0:T(1024)} %bitcast.15) | data formatting | bytes 147456
